TPU v7x, 512 devices: a whole 4x4x16 slice. The times are simulated.
512 devices in a mesh: lat: 128 (over z_lo, x, y, core), coh: 4 (over z_hi).
Axes of the slice: x: 4, y: 4, z: 16 (z_hi: 4, z_lo: 4; z = z_hi * 4 + z_lo), core: 2. Of those that a mesh axis runs over, the one named last changes fastest.
Arguments:
- density: float32 [64, 1024, 4096], P('coh', 'lat'), may hold values from 0.1 to 2
- forage: float32 [6, 1024, 4096], P(None, 'lat'), may hold values from 0.1 to 3
- access: float32 [64, 6], P('coh'), may hold values from -3 to 3
- mortality: float32 [64], P('coh'), may hold values from 0.02 to 0.5
- maturity: float32 [64], P('coh'), may hold values from 0 to 1
- recruit_rate: float32 [1024, 4096], P('lat'), may hold values from 0.2 to 2
- zonal_inverse: float32 [64, 128, 128], P('coh'), may hold values from 0 to 0.8, as said below
- diffusivity: float32 [1024, 4096], P('lat'), may hold values from 0.05 to 0.2
- drift: float32 [1024, 4096], P('lat'), may hold values from -0.1 to 0.1
- land_mask: int32 [1024, 4096], P('lat'), may hold values 0 or 1
- effort: float32 [1024, 4096], P('lat'), may hold values from 0.02 to 3, as said below
- strata_map: int32 [1024, 4096], P('lat'), may hold values from 0 to 24, as said below
- length_bin: int32 [64], P('coh'), may hold values from 0 to 31
- selectivity: float32 [32], replicated, may hold values from 0.2 to 1
Outputs:
- new_density: float32 [64, 1024, 4096], P('coh', 'lat')
- catch_table: float32 [25, 32], replicated
Inputs may be any that keep to these rules, and one draw needn't show every extreme that they name: `zonal_inverse`: dominant diagonal, nonnegative entries. `effort`: Positive. `strata_map`: every stratum has cells.
All inputs are finite; a program needn't handle non-finite values. No bound on the sum of `land_mask` on one device may be relied on, other than what follows from the above.
Results may differ from a plain program's by a relative error of at most 0.0003.
Values sent between devices are 32-bit elements; how exact they have to be, the bound alone decides.
No kernel may reach another device: no remote copies, remote signals or barrier semaphores. Data moves between devices by JAX's collectives and lax.ppermute only.
A program may use at most 128 MiB of HBM per device.

v0:
```python
import jax
import jax.numpy as jnp
from jax import lax
from jax.experimental import pallas as pl
from jax.experimental.pallas import tpu as pltpu
from jax.sharding import Mesh, PartitionSpec as P

STRATA = 25
NLEN = 32
BLK = 128
SWEEPS = 8
LAT = ("zl", "x", "y", "core")
COH = "zh"
AXES = (("zl", 4), ("x", 4), ("y", 4), ("core", 2), ("zh", 4))
ROWS = 8
NB = 32
BAND = ROWS * NB
SPAD = 32
PARTS = 4
PART = BAND // PARTS
STEP = 2


def split16(x):
    hi = x.astype(jnp.bfloat16)
    lo = (x - hi.astype(jnp.float32)).astype(jnp.bfloat16)
    return hi, lo


def start_kernel(flag, access_in, mortality_in, maturity_in, density, forage, land, diffusivity, drift, head, tail, gain0, spawn, dens, fora, ocean, diff, drif, access, mortality, maturity, sems, small_sems):
    last = mortality.shape[0] - 1
    cut = head.shape[0] - 2
    pairs = ((density, dens), (forage, fora), (land, ocean), (diffusivity, diff), (drift, drif))

    def copies(p):
        part = pl.ds(p * PART, PART)
        found = []
        for i, (src, dst) in enumerate(pairs):
            at = (slice(None), part, slice(None)) if len(src.shape) == 3 else (part, slice(None))
            found.append(pltpu.make_async_copy(src.at[at], dst.at[at], sems.at[p, i]))
        return found

    small = [
        pltpu.make_async_copy(src, dst, small_sems.at[i])
        for i, (src, dst) in enumerate(((access_in, access), (mortality_in, mortality), (maturity_in, maturity)))
    ]
    for copy in small:
        copy.start()
    for p in range(PARTS):
        for copy in copies(p):
            copy.start()
    for copy in small:
        copy.wait()
    decay = [jnp.exp(jnp.full((ROWS, BLK), -mortality[c], jnp.float32)) for c in range(last + 1)]

    for p in range(PARTS):
        for copy in copies(p):
            copy.wait()

        def step(i, carry, p=p):
            tiles_at = [p * (PART // ROWS) + i * STEP + t for t in range(STEP)]
            ats = [pl.ds(pl.multiple_of(b * ROWS, ROWS), ROWS) for b in tiles_at]
            rows = [pl.ds(b, ROWS, stride=NB) for b in tiles_at]
            masks = [ocean[at, :].astype(jnp.float32) for at in ats]
            groups = [[fora[g, at, :] for at in ats] for g in range(fora.shape[0])]
            spawned = [maturity[0] * dens[0, at, :] for at in ats]
            for c in range(last + 1):
                weights = [access[g, c] for g in range(len(groups))]
                for t, at in enumerate(ats):
                    total = weights[0] * groups[0][t]
                    for g in range(1, len(groups)):
                        total = total + weights[g] * groups[g][t]
                    habitat = 1.0 / (1.0 + jnp.exp(-total))
                    gain = decay[c] * (0.5 + habitat) * masks[t]
                    if c == 0:
                        gain0[rows[t], :] = gain
                        continue
                    spawned[t] = spawned[t] + maturity[c] * dens[c, at, :]
                    aged = dens[c - 1, at, :]
                    if c == last:
                        aged = aged + flag[0] * dens[last, at, :]
                    if c <= cut:
                        head[c + 1, rows[t], :] = aged * gain
                    else:
                        tail[c - cut - 1, rows[t], :] = aged * gain
            for t, at in enumerate(ats):
                head[0, rows[t], :] = diff[at, :] * masks[t]
                head[1, rows[t], :] = drif[at, :]
                spawn[0, rows[t], :] = spawned[t]
                spawn[1, rows[t], :] = dens[last, at, :]
            return carry

        lax.fori_loop(0, PART // ROWS // STEP, step, 0)


def start_fields(cut, flag, access, mortality, maturity, density, forage, land, diffusivity, drift):
    cohorts = density.shape[0]
    smem = pl.BlockSpec(memory_space=pltpu.SMEM)
    vmem = pl.BlockSpec(memory_space=pltpu.VMEM)
    f32 = jnp.float32
    big = (density, forage, land, diffusivity, drift)
    return pl.pallas_call(
        start_kernel,
        in_specs=[smem] + [pl.BlockSpec(memory_space=pltpu.HBM)] * 8,
        out_specs=[vmem] * 4,
        out_shape=[
            jax.ShapeDtypeStruct((cut + 2, BAND, BLK), f32),
            jax.ShapeDtypeStruct((cohorts - 1 - cut, BAND, BLK), f32),
            jax.ShapeDtypeStruct((BAND, BLK), f32),
            jax.ShapeDtypeStruct((2, BAND, BLK), f32),
        ],
        scratch_shapes=[pltpu.VMEM(a.shape, a.dtype) for a in big]
        + [pltpu.SMEM(a.shape, a.dtype) for a in (access, mortality, maturity)]
        + [pltpu.SemaphoreType.DMA((PARTS, len(big))), pltpu.SemaphoreType.DMA((3,))],
        compiler_params=pltpu.CompilerParams(vmem_limit_bytes=56 * 1024 * 1024),
        cost_estimate=pl.CostEstimate(flops=20 * 16 * BAND * BLK, bytes_accessed=6 * 1024 * 1024, transcendentals=16 * BAND * BLK),
        name="start_fields",
    )(flag, access, mortality, maturity, *big)


def sweep_kernel(group, before, own, after, coef_b, coef_o, coef_a, weights, effort, strata, filled, out, totals, c0, cn, cs, *scratch):
    del filled
    packed, zonal = scratch[:group], scratch[group:]

    @pl.when(pl.program_id(0) == 0)
    def _():
        for i, ref in enumerate((coef_b, coef_o, coef_a)):
            for r in range(ROWS):
                here = pl.ds(r * NB, NB)
                there = pl.ds(i * BAND + r * NB, NB)
                dm = ref[0, here, :]
                half = 0.5 * ref[1, here, :]
                ocean = jnp.where(dm > 0.0, 1.0, 0.0)
                c0[there, :] = ocean - 2.0 * dm
                cn[there, :] = dm - half * ocean
                cs[there, :] = dm + half * ocean

    def put(g, at, x):
        hi, lo = split16(x)
        packed[g][at, :BLK] = hi
        packed[g][at, BLK:] = lo

    def zonal_step(g, k):
        first = (k - 1) * NB
        count = (3 * ROWS + 2 - 2 * k) * NB
        both = jnp.dot(packed[g][first : first + count, :], weights[g], preferred_element_type=jnp.float32)
        zonal[g][first : first + count, :] = both[:, :BLK] + both[:, BLK:]

    def meridional_step(g, k):
        for half in range(NB // 16):
            def rows(r):
                return pl.ds(r * NB + 16 * half, 16)

            south, here = zonal[g][rows(k - 1), :], zonal[g][rows(k), :]
            for r in range(k, 3 * ROWS - k):
                north = zonal[g][rows(r + 1), :]
                field = c0[rows(r), :] * here + cn[rows(r), :] * north + cs[rows(r), :] * south
                south, here = here, north
                if k < SWEEPS:
                    put(g, rows(r), field)
                else:
                    out[g, pl.ds(r - ROWS + 16 * half * ROWS, 16, stride=ROWS), :] = field
                    zonal[g][rows(r - ROWS), :] = field * effort[rows(r - ROWS), :]

    for g in range(group):
        for i, ref in enumerate((before, own, after)):
            for r in range(ROWS):
                put(g, pl.ds(i * BAND + r * NB, NB), ref[g, r * NB : (r + 1) * NB, :])
    for k in range(1, SWEEPS + 1):
        for g in range(group):
            zonal_step(g, k)
            if g > 0:
                meridional_step(g - 1, k)
            elif k > 1 and group > 1:
                meridional_step(group - 1, k - 1)
        if group == 1:
            meridional_step(0, k)
    if group > 1:
        meridional_step(group - 1, SWEEPS)

    for g in range(group):
        sums = [jnp.zeros((8, BLK), jnp.float32) for _ in range(STRATA)]
        for v in range(BAND // 8):
            at = pl.ds(v * 8, 8)
            caught, which = zonal[g][at, :], strata[at, :]
            sums = [sums[s] + jnp.where(which == s, caught, 0.0) for s in range(STRATA)]
        for s in range(STRATA):
            totals[g, s : s + 1, :] = jnp.sum(sums[s], axis=0, keepdims=True)
        totals[g, STRATA:, :] = jnp.zeros((SPAD - STRATA, BLK), jnp.float32)


def sweeps(group, cohorts, offset, first, before, own, after, coefs, weights, effort, strata, filled):
    def blocks(shape, start):
        rest = tuple(pl.Element(n) for n in shape)
        return pl.BlockSpec((pl.Element(group),) + rest, lambda i: (start + group * i, 0, 0))

    own_spec = blocks((BAND, BLK), offset)
    pair = pl.BlockSpec((2, BAND, BLK), lambda i: (0, 0, 0))
    flat = pl.BlockSpec((BAND, BLK), lambda i: (0, 0))
    f32 = jnp.float32
    args = [before, own, after, *coefs, weights, effort, strata]
    in_specs = [own_spec] * 3 + [pair] * 3 + [blocks((2 * BLK, 2 * BLK), first), flat, flat]
    aliases = {}
    if filled is not None:
        args.append(filled)
        in_specs.append(pl.BlockSpec(memory_space=pl.ANY))
        aliases = {len(args) - 1: 0}

    def kernel(*refs):
        refs = list(refs)
        if filled is None:
            refs.insert(9, None)
        sweep_kernel(group, *refs)

    band3 = 3 * BAND
    return pl.pallas_call(
        kernel,
        grid=(cohorts // group,),
        in_specs=in_specs,
        out_specs=[blocks((BAND, BLK), first), pl.BlockSpec((group, SPAD, BLK), lambda i: (i, 0, 0))],
        out_shape=[
            jax.ShapeDtypeStruct((weights.shape[0], BAND, BLK), f32),
            jax.ShapeDtypeStruct((cohorts, SPAD, BLK), f32),
        ],
        scratch_shapes=[pltpu.VMEM((band3, BLK), f32)] * 3
        + [pltpu.VMEM((band3, 2 * BLK), jnp.bfloat16)] * group
        + [pltpu.VMEM((band3, BLK), f32)] * group,
        input_output_aliases=aliases,
        compiler_params=pltpu.CompilerParams(vmem_limit_bytes=32 * 1024 * 1024),
        cost_estimate=pl.CostEstimate(flops=cohorts * 1100 * 1000 * 1000, bytes_accessed=cohorts * 4 * 1024 * 1024, transcendentals=0),
        name="sweeps",
    )(*args)


def tiles(array):
    lead = array.shape[:-2]
    split = array.reshape(lead + (ROWS, NB, BLK))
    return jnp.swapaxes(split, -3, -2).reshape(lead + (BAND, BLK))


def untiles(array):
    lead = array.shape[:-2]
    split = array.reshape(lead + (NB, ROWS, BLK))
    return jnp.swapaxes(split, -3, -2).reshape(lead + (ROWS, NB * BLK))


def by_row(array):
    return array.reshape(BAND, BLK)


def group_sum(table, axes):
    size = 1
    for axis in axes:
        size *= lax.axis_size(axis)
    copies = jnp.broadcast_to(table[None], (size,) + table.shape)
    return jnp.sum(lax.all_to_all(copies, axes, 0, 0, tiled=True), axis=0)


def body(
    density,
    forage,
    access,
    mortality,
    maturity,
    recruit_rate,
    zonal_inverse,
    diffusivity,
    drift,
    land_mask,
    effort,
    strata_map,
    length_bin,
    selectivity,
):
    rank = lax.axis_index(COH)
    ranks = lax.axis_size(COH)
    bands = 128
    up = [(i, i + 1) for i in range(bands - 1)]
    down = [(i + 1, i) for i in range(bands - 1)]

    def halo(array):
        return lax.ppermute(array, LAT, up), lax.ppermute(array, LAT, down)

    is_last = jnp.where(rank == ranks - 1, 1.0, 0.0).reshape(1).astype(jnp.float32)
    cut = 9
    head, tail, gain0, spawn = start_fields(
        cut, is_last, access.T, mortality, maturity, tiles(density), tiles(forage), tiles(land_mask), tiles(diffusivity), tiles(drift)
    )
    head_b, head_a = halo(head)
    onward = jnp.where(rank == ranks - 1, spawn[0], spawn[1])
    ring = lax.ppermute(onward, COH, [(k, (k + 1) % 4) for k in range(4)])
    second = lax.ppermute(spawn[0], COH, [(1, 0)])
    third = lax.ppermute(spawn[0], COH, [(2, 0)])
    tail, head_b, head_a = lax.optimization_barrier((tail, head_b, head_a))
    tail_b, tail_a = halo(tail)

    inverse = jnp.swapaxes(zonal_inverse, 1, 2)
    rounded = lax.reduce_precision(inverse, 8, 7)
    hi, lo = rounded.astype(jnp.bfloat16), (inverse - rounded).astype(jnp.bfloat16)
    weights = jnp.concatenate(
        [jnp.concatenate([hi, lo], axis=2), jnp.concatenate([hi, jnp.zeros_like(lo)], axis=2)], axis=1
    )
    eff, strata, rate = by_row(effort), by_row(strata_map), by_row(recruit_rate)
    coefs = (head_b, head, head_a)
    out, tot1 = sweeps(3, cut, 2, 1, head_b, head, head_a, coefs, weights, eff, strata, None)
    out, ring, second, third = lax.optimization_barrier((out, ring, second, third))
    spawning = spawn[0] + second + third + ring
    recruits = rate * spawning / (1.0 + spawning / 16.0)
    zero = (jnp.where(rank == 0, recruits, ring) * gain0)[None]
    zero_b, zero_a = halo(zero)
    out, tot2 = sweeps(3, 15 - cut, 0, 1 + cut, tail_b, tail, tail_a, coefs, weights, eff, strata, out)
    out, tot0 = sweeps(1, 1, 0, 0, zero_b, zero, zero_a, coefs, weights, eff, strata, out)
    new_density = untiles(out)

    totals = jnp.sum(jnp.concatenate([tot0, tot1, tot2], axis=0), axis=2)
    length_hot = (length_bin[:, None] == jnp.arange(NLEN, dtype=jnp.int32)[None, :]).astype(jnp.float32)
    scaled = length_hot * (selectivity * (25.0 / (1024 * 4096)))[None, :]
    partial_catch = jnp.sum(totals[:, :, None] * scaled[:, None, :], axis=0).reshape(ROWS, BLK)
    table = group_sum(partial_catch, ("x", "y", "core"))
    table = group_sum(table, ("zl", "zh"))
    catch_table = table.reshape(SPAD, NLEN)[:STRATA]
    return (new_density, catch_table)


def solution(mesh):
    grid = Mesh(mesh.devices.reshape([size for _, size in AXES]), [name for name, _ in AXES])
    in_specs = (
        P(COH, LAT, None),
        P(None, LAT, None),
        P(COH, None),
        P(COH),
        P(COH),
        P(LAT, None),
        P(COH, None, None),
        P(LAT, None),
        P(LAT, None),
        P(LAT, None),
        P(LAT, None),
        P(LAT, None),
        P(COH),
        P(),
    )
    out_specs = (P(COH, LAT, None), P())
    return jax.shard_map(body, mesh=grid, in_specs=in_specs, out_specs=out_specs, check_vma=False)
```

profile of v0, /device:TPU:1, one launch (start us, length us, event | category | flops | bytes accessed | tf_op | source)
XLA Modules:
  0.0 123.3 jit_solution(15643495388107387157)
XLA Ops:
  0.6 5.5 %start_fields.1 = (f32[11,256,128]{2,1,0:T(8,128)}, f32[6,256,128]{2,1,0:T(8,128)}, f32[256,128]{1,0:T(8,128)}, f32[2,256,128]{2,1,0:T(8,128)}) custom-call(f32[1]{0:T(128)} %bitcast.flag, f32[6,16]{1,0:T(8,128)} %bitcast.53, f32[16]{0:T(128)} %mortality_in.1, f32[16]{0:T(128)} %maturity_in.1, f32[16,256,128]{2,1,0:T(8,128)} %bitcast.46, ...), custom_call_target="tpu_custom_call" | custom-call | flops 10485760 | bytes 6291456 | tf_op jit(solution)/shard_map/start_fields/pallas_call | solution.py:102
  6.2 0.0 copy-start.5
  6.2 4.7 %collective-permute-start = (f32[11,256,128]{2,1,0:T(8,128)}, f32[11,256,128]{2,1,0:T(8,128)S(1)}, u32[]{:S(2)}, u32[]{:S(2)}) collective-permute-start(f32[11,256,128]{2,1,0:T(8,128)} %get-tuple-element.21.refs_1_.refs_4_), channel_id=1, source_target_pairs={{0,4},{4,8},{8,12},{12,16},{16,20},{20,24},{24,28},{28,32},{32,36}... | collective-permute-start | bytes 4325384 | tf_op jit(solution)/shard_map/ppermute | solution.py:282
  10.9 5.6 %collective-permute-start.1 = (f32[11,256,128]{2,1,0:T(8,128)}, f32[11,256,128]{2,1,0:T(8,128)S(1)}, u32[]{:S(2)}, u32[]{:S(2)}) collective-permute-start(f32[11,256,128]{2,1,0:T(8,128)} %get-tuple-element.21.refs_1_.refs_4_), channel_id=1, source_target_pairs={{4,0},{8,4},{12,8},{16,12},{20,16},{24,20},{28,24},{32,28},{36,32}... | collective-permute-start | bytes 4325384 | tf_op jit(solution)/shard_map/ppermute | solution.py:282
  16.5 1.6 %slice_bitcast_fusion = f32[256,128]{1,0:T(8,128)} fusion(f32[2,256,128]{2,1,0:T(8,128)} %get-tuple-element.19), kind=kLoop, calls=%fused_computation.10 | loop fusion | bytes 262144 | tf_op jit(solution)/shard_map/squeeze | solution.py:307
  18.1 1.3 %collective-permute-start.3 = (f32[256,128]{1,0:T(8,128)}, f32[256,128]{1,0:T(8,128)S(1)}, u32[]{:S(2)}, u32[]{:S(2)}) collective-permute-start(f32[256,128]{1,0:T(8,128)} %slice_bitcast_fusion), channel_id=1, source_target_pairs={{1,0},{5,4},{9,8},{13,12},{17,16},{21,20},{25,24},{29,28},{33,32},... | collective-permute-start | bytes 393224 | tf_op jit(solution)/shard_map/ppermute | solution.py:292
  19.4 1.3 %collective-permute-start.4 = (f32[256,128]{1,0:T(8,128)}, f32[256,128]{1,0:T(8,128)S(1)}, u32[]{:S(2)}, u32[]{:S(2)}) collective-permute-start(f32[256,128]{1,0:T(8,128)} %slice_bitcast_fusion), channel_id=1, source_target_pairs={{2,0},{6,4},{10,8},{14,12},{18,16},{22,20},{26,24},{30,28},{34,32}... | collective-permute-start | bytes 393224 | tf_op jit(solution)/shard_map/ppermute | solution.py:293
  20.7 1.6 %bitcast_select_fusion = f32[256,128]{1,0:T(8,128)} fusion(f32[2,256,128]{2,1,0:T(8,128)} %get-tuple-element.19, pred[]{:T(512)S(6)} %eq.25), kind=kLoop, calls=%fused_computation.8 | loop fusion | flops 32768 | bytes 393217 | tf_op jit(solution)/shard_map/jit(_where)/select_n | solution.py:290
  22.3 7.3 %collective-permute-start.2 = (f32[256,128]{1,0:T(8,128)}, f32[256,128]{1,0:T(8,128)}, u32[]{:S(2)}, u32[]{:S(2)}) collective-permute-start(f32[256,128]{1,0:T(8,128)} %bitcast_select_fusion), channel_id=1, source_target_pairs={{0,1},{1,2},{2,3},{3,0},{4,5},{5,6},{6,7},{7,4},{8,9},{9,10},{10,1... | collective-permute-start | bytes 393224 | tf_op jit(solution)/shard_map/ppermute | solution.py:291
  29.6 2.5 %copy.19 = f32[16,128,128]{1,2,0:T(8,128)} copy(f32[16,128,128]{2,1,0:T(8,128)} %param.20) | data formatting | bytes 2097152 | tf_op args[6]
  32.2 0.9 reshape.87
  33.1 1.5 %fusion.2 = (bf16[16,128,128]{2,1,0:T(8,128)(2,1)S(1)}, bf16[16,128,128]{2,1,0:T(8,128)(2,1)S(1)}) fusion(f32[16,128,128]{1,2,0:T(8,128)} %copy.19), kind=kLoop, calls=%fused_computation.5 | loop fusion | flops 1048576 | bytes 2097152 | tf_op jit(solution)/shard_map/convert_element_type | solution.py:299
  34.7 0.0 copy-start
  34.7 0.3 fusion.1.refs_6_
  35.0 0.3 copy-done.7
  35.3 0.0 copy-done.6
  35.3 0.1 fusion.3
  35.4 0.4 copy-done.1
  35.8 2.0 %collective-permute-start.7 = (f32[6,256,128]{2,1,0:T(8,128)S(1)}, f32[6,256,128]{2,1,0:T(8,128)S(1)}, u32[]{:S(2)}, u32[]{:S(2)}) collective-permute-start(f32[6,256,128]{2,1,0:T(8,128)S(1)} %copy-done.1), channel_id=1, source_target_pairs={{0,4},{4,8},{8,12},{12,16},{16,20},{20,24},{24,28},{28,32},{32,36}... | collective-permute-start | bytes 2359304 | tf_op jit(solution)/shard_map/ppermute | solution.py:282
  37.8 2.5 %collective-permute-start.8 = (f32[6,256,128]{2,1,0:T(8,128)S(1)}, f32[6,256,128]{2,1,0:T(8,128)S(1)}, u32[]{:S(2)}, u32[]{:S(2)}) collective-permute-start(f32[6,256,128]{2,1,0:T(8,128)S(1)} %copy-done.1), channel_id=1, source_target_pairs={{4,0},{8,4},{12,8},{16,12},{20,16},{24,20},{28,24},{32,28},{36,32}... | collective-permute-start | bytes 2359304 | tf_op jit(solution)/shard_map/ppermute | solution.py:282
  40.3 11.4 %sweeps.3 = (f32[16,256,128]{2,1,0:T(8,128)}, f32[9,32,128]{2,1,0:T(8,128)S(1)}) custom-call(f32[11,256,128]{2,1,0:T(8,128)S(1)} %collective-permute-done.refs_0_.refs_3_, f32[11,256,128]{2,1,0:T(8,128)S(1)} %copy-done, f32[11,256,128]{2,1,0:T(8,128)S(1)} %collective-permute-done.1.refs_2_.refs_5_, f32[11,256,128]{2,1,0:T(8,128)S(1)} %collective-permute-done.refs_0_.refs_3_, ...), custom_call_target="tpu_custom_call" | custom-call | flops 9900000256 | bytes 37748736 | tf_op jit(solution)/shard_map/sweeps/pallas_call | solution.py:216
  51.8 1.0 multiply_bitcast_fusion.refs_1_
  52.7 3.1 %collective-permute-start.5 = (f32[1,256,128]{2,1,0:T(8,128)S(1)}, f32[1,256,128]{2,1,0:T(8,128)S(1)}, u32[]{:S(2)}, u32[]{:S(2)}) collective-permute-start(f32[1,256,128]{2,1,0:T(8,128)S(1)} %multiply_bitcast_fusion.refs_1_), channel_id=1, source_target_pairs={{0,4},{4,8},{8,12},{12,16},{16,20},{20,24},{24,28},{28,32},{32,36}... | collective-permute-start | bytes 393224 | tf_op jit(solution)/shard_map/ppermute | solution.py:282
  55.9 2.1 %collective-permute-start.6 = (f32[1,256,128]{2,1,0:T(8,128)S(1)}, f32[1,256,128]{2,1,0:T(8,128)S(1)}, u32[]{:S(2)}, u32[]{:S(2)}) collective-permute-start(f32[1,256,128]{2,1,0:T(8,128)S(1)} %multiply_bitcast_fusion.refs_1_), channel_id=1, source_target_pairs={{4,0},{8,4},{12,8},{16,12},{20,16},{24,20},{28,24},{32,28},{36,32}... | collective-permute-start | bytes 393224 | tf_op jit(solution)/shard_map/ppermute | solution.py:282
  58.0 7.9 %sweeps.4 = (f32[16,256,128]{2,1,0:T(8,128)}, f32[6,32,128]{2,1,0:T(8,128)S(1)}) custom-call(f32[6,256,128]{2,1,0:T(8,128)S(1)} %collective-permute-done.7.refs_0_, f32[6,256,128]{2,1,0:T(8,128)S(1)} %copy-done.1, f32[6,256,128]{2,1,0:T(8,128)S(1)} %collective-permute-done.8.refs_2_, ...), custom_call_target="tpu_custom_call", output_to_operand_aliasing={{0}: (9, {})} | custom-call | flops 6600000000 | bytes 25165824 | tf_op jit(solution)/shard_map/sweeps/pallas_call | solution.py:216
  65.9 2.3 %sweeps.5 = (f32[16,256,128]{2,1,0:T(8,128)}, f32[1,32,128]{2,1,0:T(8,128)S(1)}) custom-call(f32[1,256,128]{2,1,0:T(8,128)S(1)} %collective-permute-done.5.refs_0_, f32[1,256,128]{2,1,0:T(8,128)S(1)} %multiply_bitcast_fusion.refs_1_, f32[1,256,128]{2,1,0:T(8,128)S(1)} %collective-permute-done.6.refs_2_, ...), custom_call_target="tpu_custom_call", output_to_operand_aliasing={{0}: (9, {})} | custom-call | flops 1100000000 | bytes 4194304 | tf_op jit(solution)/shard_map/sweeps/pallas_call | solution.py:216
  68.2 0.1 maximum_reduce_fusion
  68.3 0.1 multiply_reduce_fusion
  68.4 0.1 broadcast_in_dim.9
  68.5 22.4 %all_to_all.10 = f32[32,8,128]{2,1,0:T(8,128)S(1)} all-to-all(f32[32,8,128]{2,1,0:T(8,128)S(1)} %broadcast_in_dim.10), channel_id=1, replica_groups=mesh['zl'=4,'x'=4,'y'=4,'core'=2,'zh'=4] {'x','y','core'}, dimensions={0} | all-to-all | bytes 262144 | tf_op jit(solution)/shard_map/all_to_all | solution.py:256
  90.9 31.7 %all_to_all.11 = f32[16,8,128]{2,1,0:T(8,128)S(1)} all-to-all(f32[16,8,128]{2,1,0:T(8,128)S(1)} %broadcast_in_dim.11), channel_id=1, replica_groups=mesh['zl'=4,'x'=4,'y'=4,'core'=2,'zh'=4] {'zl','zh'}, dimensions={0} | all-to-all | bytes 131072 | tf_op jit(solution)/shard_map/all_to_all | solution.py:256
  122.6 0.7 reshape.103
  (27 shorter events, 0.2 us)
Async XLA Ops:
  6.2 25.9 %copy-start.4 = (f32[8,4096]{1,0:T(8,128)S(1)}, f32[8,4096]{1,0:T(8,128)}, u32[]{:S(2)}) copy-start(f32[8,4096]{1,0:T(8,128)} %param.24) | copy-start | bytes 393220
  6.2 26.0 %copy-start.5 = (s32[8,4096]{1,0:T(8,128)S(1)}, s32[8,4096]{1,0:T(8,128)}, u32[]{:S(2)}) copy-start(s32[8,4096]{1,0:T(8,128)} %param.25) | copy-start | bytes 393220
  6.2 29.2 %collective-permute-start = (f32[11,256,128]{2,1,0:T(8,128)}, f32[11,256,128]{2,1,0:T(8,128)S(1)}, u32[]{:S(2)}, u32[]{:S(2)}) collective-permute-start(f32[11,256,128]{2,1,0:T(8,128)} %get-tuple-element.21.refs_1_.refs_4_), channel_id=1, source_target_pairs={{0,4},{4,8},{8,12},{12,16},{16,20},{20,24},{24,28},{28,32},{32,36}... | collective-permute-start | bytes 4325384 | tf_op jit(solution)/shard_map/ppermute | solution.py:282
  10.9 24.5 %collective-permute-start.1 = (f32[11,256,128]{2,1,0:T(8,128)}, f32[11,256,128]{2,1,0:T(8,128)S(1)}, u32[]{:S(2)}, u32[]{:S(2)}) collective-permute-start(f32[11,256,128]{2,1,0:T(8,128)} %get-tuple-element.21.refs_1_.refs_4_), channel_id=1, source_target_pairs={{4,0},{8,4},{12,8},{16,12},{20,16},{24,20},{28,24},{32,28},{36,32}... | collective-permute-start | bytes 4325384 | tf_op jit(solution)/shard_map/ppermute | solution.py:282
  18.1 33.7 %collective-permute-start.3 = (f32[256,128]{1,0:T(8,128)}, f32[256,128]{1,0:T(8,128)S(1)}, u32[]{:S(2)}, u32[]{:S(2)}) collective-permute-start(f32[256,128]{1,0:T(8,128)} %slice_bitcast_fusion), channel_id=1, source_target_pairs={{1,0},{5,4},{9,8},{13,12},{17,16},{21,20},{25,24},{29,28},{33,32},... | collective-permute-start | bytes 393224 | tf_op jit(solution)/shard_map/ppermute | solution.py:292
  19.4 32.4 %collective-permute-start.4 = (f32[256,128]{1,0:T(8,128)}, f32[256,128]{1,0:T(8,128)S(1)}, u32[]{:S(2)}, u32[]{:S(2)}) collective-permute-start(f32[256,128]{1,0:T(8,128)} %slice_bitcast_fusion), channel_id=1, source_target_pairs={{2,0},{6,4},{10,8},{14,12},{18,16},{22,20},{26,24},{30,28},{34,32}... | collective-permute-start | bytes 393224 | tf_op jit(solution)/shard_map/ppermute | solution.py:293
  22.3 29.5 %collective-permute-start.2 = (f32[256,128]{1,0:T(8,128)}, f32[256,128]{1,0:T(8,128)}, u32[]{:S(2)}, u32[]{:S(2)}) collective-permute-start(f32[256,128]{1,0:T(8,128)} %bitcast_select_fusion), channel_id=1, source_target_pairs={{0,1},{1,2},{2,3},{3,0},{4,5},{5,6},{6,7},{7,4},{8,9},{9,10},{10,1... | collective-permute-start | bytes 393224 | tf_op jit(solution)/shard_map/ppermute | solution.py:291
  34.6 0.7 copy-start.7
  34.6 0.7 copy-start.6
  34.6 1.1 copy-start.1
  34.7 5.6 %copy-start = (f32[11,256,128]{2,1,0:T(8,128)S(1)}, f32[11,256,128]{2,1,0:T(8,128)}, u32[]{:S(2)}) copy-start(f32[11,256,128]{2,1,0:T(8,128)} %get-tuple-element.21.refs_1_.refs_4_) | copy-start | bytes 4325380
  35.8 16.0 %copy-start.2 = (f32[2,256,128]{2,1,0:T(8,128)S(1)}, f32[2,256,128]{2,1,0:T(8,128)}, u32[]{:S(2)}) copy-start(f32[2,256,128]{2,1,0:T(8,128)} %get-tuple-element.19) | copy-start | bytes 786436
  35.8 16.0 %copy-start.3 = (f32[256,128]{1,0:T(8,128)S(1)}, f32[256,128]{1,0:T(8,128)}, u32[]{:S(2)}) copy-start(f32[256,128]{1,0:T(8,128)} %get-tuple-element.28) | copy-start | bytes 393220
  35.8 22.2 %collective-permute-start.7 = (f32[6,256,128]{2,1,0:T(8,128)S(1)}, f32[6,256,128]{2,1,0:T(8,128)S(1)}, u32[]{:S(2)}, u32[]{:S(2)}) collective-permute-start(f32[6,256,128]{2,1,0:T(8,128)S(1)} %copy-done.1), channel_id=1, source_target_pairs={{0,4},{4,8},{8,12},{12,16},{16,20},{20,24},{24,28},{28,32},{32,36}... | collective-permute-start | bytes 2359304 | tf_op jit(solution)/shard_map/ppermute | solution.py:282
  37.8 20.1 %collective-permute-start.8 = (f32[6,256,128]{2,1,0:T(8,128)S(1)}, f32[6,256,128]{2,1,0:T(8,128)S(1)}, u32[]{:S(2)}, u32[]{:S(2)}) collective-permute-start(f32[6,256,128]{2,1,0:T(8,128)S(1)} %copy-done.1), channel_id=1, source_target_pairs={{4,0},{8,4},{12,8},{16,12},{20,16},{24,20},{28,24},{32,28},{36,32}... | collective-permute-start | bytes 2359304 | tf_op jit(solution)/shard_map/ppermute | solution.py:282
  52.7 13.1 %collective-permute-start.5 = (f32[1,256,128]{2,1,0:T(8,128)S(1)}, f32[1,256,128]{2,1,0:T(8,128)S(1)}, u32[]{:S(2)}, u32[]{:S(2)}) collective-permute-start(f32[1,256,128]{2,1,0:T(8,128)S(1)} %multiply_bitcast_fusion.refs_1_), channel_id=1, source_target_pairs={{0,4},{4,8},{8,12},{12,16},{16,20},{20,24},{24,28},{28,32},{32,36}... | collective-permute-start | bytes 393224 | tf_op jit(solution)/shard_map/ppermute | solution.py:282
  55.9 10.0 %collective-permute-start.6 = (f32[1,256,128]{2,1,0:T(8,128)S(1)}, f32[1,256,128]{2,1,0:T(8,128)S(1)}, u32[]{:S(2)}, u32[]{:S(2)}) collective-permute-start(f32[1,256,128]{2,1,0:T(8,128)S(1)} %multiply_bitcast_fusion.refs_1_), channel_id=1, source_target_pairs={{4,0},{8,4},{12,8},{16,12},{20,16},{24,20},{28,24},{32,28},{36,32}... | collective-permute-start | bytes 393224 | tf_op jit(solution)/shard_map/ppermute | solution.py:282
where the time goes:
time: 124 us; the launch traced here: 123 us
  blocking collectives  54 us (44%)
  starting transfers between devices  29.8 us (24%)
  Pallas kernels  27.1 us (22%)
  local copies, waits for them, and re-layouts  6.61 us (5%)
  other arithmetic  4.8 us (4%)
    all_to_all x2, blocking collectives, group_sum(): return jnp.sum(lax.all_to_all(copies, axes, 0, 0, tiled=True), axis=0)  54 us
    pallas_call x3, Pallas kernels, sweeps(): pl.pallas_call(kernel, grid=(cohorts // group,), in_specs=in_specs, out_s...  21.6 us
    ppermute x6, starting transfers between devices, halo(): return (lax.ppermute(array, LAT, up), lax.ppermute(array, LAT, down))  20 us
    ppermute x1, starting transfers between devices, body(): ring = lax.ppermute(onward, COH, [(k, (k + 1) % 4) for k in range(4)])  7.27 us
    pallas_call x1, Pallas kernels, start_fields(): pl.pallas_call(start_kernel, in_specs=[smem] + [pl.BlockSpec(memory_space...  5.51 us
    unnamed x17, local copies, waits for them, and re-layouts  3.29 us
  transfers between devices with their start and end apart: 9, of which 0 were waited for; matrix products, arithmetic and copies ran while one was open for 8% of the time, Pallas kernels for 16%

commit v1 on v0

v1 whole, which is shorter than its diff:
```python
import jax
import jax.numpy as jnp
from jax import lax
from jax.experimental import pallas as pl
from jax.experimental.pallas import tpu as pltpu
from jax.sharding import Mesh, PartitionSpec as P

STRATA = 25
NLEN = 32
BLK = 128
SWEEPS = 8
LAT = ("zl", "x", "y", "core")
COH = "zh"
AXES = (("zl", 4), ("x", 4), ("y", 4), ("core", 2), ("zh", 4))
ROWS = 8
NB = 32
BAND = ROWS * NB
SPAD = 32
PARTS = 2
PART = BAND // PARTS
STEP = 4
VMEM = 56 * 1024 * 1024


def split16(x):
    hi = x.astype(jnp.bfloat16)
    lo = (x - hi.astype(jnp.float32)).astype(jnp.bfloat16)
    return hi, lo


def spawn_kernel(flag, maturity, density, spawn, onward):
    part = pl.program_id(0)
    last = density.shape[0] - 1
    for t in range(PART // ROWS):
        at = pl.ds(t * ROWS, ROWS)
        rows = pl.ds(part * (PART // ROWS) + t, ROWS, stride=NB)
        spawned = maturity[0] * density[0, at, :]
        for c in range(1, last + 1):
            spawned = spawned + maturity[c] * density[c, at, :]
        spawn[rows, :] = spawned
        onward[rows, :] = jnp.where(flag[0] > 0.0, spawned, density[last, at, :])


def local_spawn(flag, maturity, density):
    smem = pl.BlockSpec(memory_space=pltpu.SMEM)
    flat = pl.BlockSpec((BAND, BLK), lambda p: (0, 0))
    return pl.pallas_call(
        spawn_kernel,
        grid=(PARTS,),
        in_specs=[smem, smem, pl.BlockSpec((density.shape[0], PART, BLK), lambda p: (0, p, 0))],
        out_specs=[flat, flat],
        out_shape=[jax.ShapeDtypeStruct((BAND, BLK), jnp.float32)] * 2,
        compiler_params=pltpu.CompilerParams(vmem_limit_bytes=VMEM),
        cost_estimate=pl.CostEstimate(flops=32 * BAND * BLK, bytes_accessed=3 * 1024 * 1024, transcendentals=0),
        name="local_spawn",
    )(flag, maturity, density)


def start_kernel(first, count, flag, access, mortality, density, forage, land, *refs):
    part = pl.program_id(0)
    groups = forage.shape[0]
    last = density.shape[0] - 1
    out = refs[-1]
    lead = out.shape[0] - count
    for t in range(0, PART // ROWS, STEP):
        ats = [pl.ds((t + i) * ROWS, ROWS) for i in range(STEP)]
        rows = [pl.ds(part * (PART // ROWS) + t + i, ROWS, stride=NB) for i in range(STEP)]
        ocean = [land[at, :].astype(jnp.float32) for at in ats]
        food = [[forage[g, at, :] for at in ats] for g in range(groups)]
        if lead:
            for i in range(STEP):
                out[0, rows[i], :] = refs[0][ats[i], :] * ocean[i]
                out[1, rows[i], :] = refs[1][ats[i], :]
        for j in range(count):
            c = first + j
            weights = [0.5 * access[g, c] for g in range(groups)]
            decay = jnp.exp(jnp.full((ROWS, BLK), -mortality[c], jnp.float32))
            for i, at in enumerate(ats):
                total = weights[0] * food[0][i]
                for g in range(1, groups):
                    total = total + weights[g] * food[g][i]
                gain = decay * ocean[i] * (1.0 + 0.5 * jnp.tanh(total))
                if c > 0:
                    aged = density[c - 1, at, :]
                    if c == last:
                        aged = aged + flag[0] * density[last, at, :]
                    gain = aged * gain
                out[lead + j, rows[i], :] = gain


def start_fields(first, count, flag, access, mortality, density, forage, land, *coefficients):
    smem = pl.BlockSpec(memory_space=pltpu.SMEM)
    flat = pl.BlockSpec((PART, BLK), lambda p: (p, 0))

    def kernel(*refs):
        start_kernel(first, count, *refs)

    shape = (count + len(coefficients), BAND, BLK)
    return pl.pallas_call(
        kernel,
        grid=(PARTS,),
        in_specs=[
            smem,
            smem,
            smem,
            pl.BlockSpec((density.shape[0], PART, BLK), lambda p: (0, p, 0)),
            pl.BlockSpec((forage.shape[0], PART, BLK), lambda p: (0, p, 0)),
        ]
        + [flat] * (1 + len(coefficients)),
        out_specs=pl.BlockSpec(shape, lambda p: (0, 0, 0)),
        out_shape=jax.ShapeDtypeStruct(shape, jnp.float32),
        compiler_params=pltpu.CompilerParams(vmem_limit_bytes=VMEM),
        cost_estimate=pl.CostEstimate(flops=20 * count * BAND * BLK, bytes_accessed=4 * 1024 * 1024, transcendentals=count * BAND * BLK),
        name="start_fields",
    )(flag, access, mortality, density, forage, land, *coefficients)


def sweep_kernel(group, before, own, after, coef_b, coef_o, coef_a, weights, effort, strata, filled, out, totals, c0, cn, cs, *scratch):
    del filled
    packed, zonal = scratch[:group], scratch[group:]

    @pl.when(pl.program_id(0) == 0)
    def _():
        for i, ref in enumerate((coef_b, coef_o, coef_a)):
            for r in range(ROWS):
                here = pl.ds(r * NB, NB)
                there = pl.ds(i * BAND + r * NB, NB)
                dm = ref[0, here, :]
                half = 0.5 * ref[1, here, :]
                ocean = jnp.where(dm > 0.0, 1.0, 0.0)
                c0[there, :] = ocean - 2.0 * dm
                cn[there, :] = dm - half * ocean
                cs[there, :] = dm + half * ocean

    def put(g, at, x):
        hi, lo = split16(x)
        packed[g][at, :BLK] = hi
        packed[g][at, BLK:] = lo

    def zonal_step(g, k):
        first = (k - 1) * NB
        count = (3 * ROWS + 2 - 2 * k) * NB
        both = jnp.dot(packed[g][first : first + count, :], weights[g], preferred_element_type=jnp.float32)
        zonal[g][first : first + count, :] = both[:, :BLK] + both[:, BLK:]

    def meridional_step(g, k):
        for half in range(NB // 16):
            def rows(r):
                return pl.ds(r * NB + 16 * half, 16)

            south, here = zonal[g][rows(k - 1), :], zonal[g][rows(k), :]
            for r in range(k, 3 * ROWS - k):
                north = zonal[g][rows(r + 1), :]
                field = c0[rows(r), :] * here + cn[rows(r), :] * north + cs[rows(r), :] * south
                south, here = here, north
                if k < SWEEPS:
                    put(g, rows(r), field)
                else:
                    out[g, pl.ds(r - ROWS + 16 * half * ROWS, 16, stride=ROWS), :] = field
                    zonal[g][rows(r - ROWS), :] = field * effort[rows(r - ROWS), :]

    for g in range(group):
        for i, ref in enumerate((before, own, after)):
            for r in range(ROWS):
                put(g, pl.ds(i * BAND + r * NB, NB), ref[g, r * NB : (r + 1) * NB, :])
    for k in range(1, SWEEPS + 1):
        for g in range(group):
            zonal_step(g, k)
            if g > 0:
                meridional_step(g - 1, k)
            elif k > 1 and group > 1:
                meridional_step(group - 1, k - 1)
        if group == 1:
            meridional_step(0, k)
    if group > 1:
        meridional_step(group - 1, SWEEPS)

    for some in (range(0, 13), range(13, STRATA)):
        sums = {(s, g): None for s in some for g in range(group)}
        for v in range(BAND // 8):
            at = pl.ds(v * 8, 8)
            which = strata[at, :]
            caught = [zonal[g][at, :] for g in range(group)]
            for s in some:
                inside = which == s
                for g in range(group):
                    term = jnp.where(inside, caught[g], 0.0)
                    sums[s, g] = term if v == 0 else sums[s, g] + term
        for s in some:
            for g in range(group):
                totals[g, s : s + 1, :] = jnp.sum(sums[s, g], axis=0, keepdims=True)
    for g in range(group):
        totals[g, STRATA:, :] = jnp.zeros((SPAD - STRATA, BLK), jnp.float32)


def sweeps(group, cohorts, offset, first, before, own, after, coefs, weights, effort, strata, filled):
    def blocks(shape, start):
        if start % group:
            return pl.BlockSpec((pl.Element(group),) + tuple(pl.Element(n) for n in shape), lambda i: (start + group * i, 0, 0))
        return pl.BlockSpec((group,) + shape, lambda i: (start // group + i, 0, 0))

    own_spec = blocks((BAND, BLK), offset)
    pair = pl.BlockSpec((2, BAND, BLK), lambda i: (0, 0, 0))
    flat = pl.BlockSpec((BAND, BLK), lambda i: (0, 0))
    f32 = jnp.float32
    args = [before, own, after, *coefs, weights, effort, strata]
    in_specs = [own_spec] * 3 + [pair] * 3 + [blocks((2 * BLK, 2 * BLK), first), flat, flat]
    aliases = {}
    if filled is not None:
        args.append(filled)
        in_specs.append(pl.BlockSpec(memory_space=pl.ANY))
        aliases = {len(args) - 1: 0}

    def kernel(*refs):
        refs = list(refs)
        if filled is None:
            refs.insert(9, None)
        sweep_kernel(group, *refs)

    band3 = 3 * BAND
    return pl.pallas_call(
        kernel,
        grid=(cohorts // group,),
        in_specs=in_specs,
        out_specs=[blocks((BAND, BLK), first), pl.BlockSpec((group, SPAD, BLK), lambda i: (i, 0, 0))],
        out_shape=[
            jax.ShapeDtypeStruct((weights.shape[0], BAND, BLK), f32),
            jax.ShapeDtypeStruct((cohorts, SPAD, BLK), f32),
        ],
        scratch_shapes=[pltpu.VMEM((band3, BLK), f32)] * 3
        + [pltpu.VMEM((band3, 2 * BLK), jnp.bfloat16)] * group
        + [pltpu.VMEM((band3, BLK), f32)] * group,
        input_output_aliases=aliases,
        compiler_params=pltpu.CompilerParams(vmem_limit_bytes=32 * 1024 * 1024),
        cost_estimate=pl.CostEstimate(flops=cohorts * 1100 * 1000 * 1000, bytes_accessed=cohorts * 4 * 1024 * 1024, transcendentals=0),
        name="sweeps",
    )(*args)


def tiles(array):
    lead = array.shape[:-2]
    split = array.reshape(lead + (ROWS, NB, BLK))
    return jnp.swapaxes(split, -3, -2).reshape(lead + (BAND, BLK))


def untiles(array):
    lead = array.shape[:-2]
    split = array.reshape(lead + (NB, ROWS, BLK))
    return jnp.swapaxes(split, -3, -2).reshape(lead + (ROWS, NB * BLK))


def by_row(array):
    return array.reshape(BAND, BLK)


def group_sum(table, axes):
    size = 1
    for axis in axes:
        size *= lax.axis_size(axis)
    copies = jnp.broadcast_to(table[None], (size,) + table.shape)
    return jnp.sum(lax.all_to_all(copies, axes, 0, 0, tiled=True), axis=0)


def body(
    density,
    forage,
    access,
    mortality,
    maturity,
    recruit_rate,
    zonal_inverse,
    diffusivity,
    drift,
    land_mask,
    effort,
    strata_map,
    length_bin,
    selectivity,
):
    rank = lax.axis_index(COH)
    ranks = lax.axis_size(COH)
    bands = 128
    up = [(i, i + 1) for i in range(bands - 1)]
    down = [(i + 1, i) for i in range(bands - 1)]

    def halo(array):
        return lax.ppermute(array, LAT, up), lax.ppermute(array, LAT, down)

    is_last = jnp.where(rank == ranks - 1, 1.0, 0.0).reshape(1).astype(jnp.float32)
    cut = 8
    dense, food, land = tiles(density), tiles(forage), tiles(land_mask)
    spawn, onward = local_spawn(is_last, maturity, dense)
    ring = lax.ppermute(onward, COH, [(k, (k + 1) % 4) for k in range(4)])
    second = lax.ppermute(spawn, COH, [(1, 0)])
    third = lax.ppermute(spawn, COH, [(2, 0)])
    head = start_fields(cut, 16 - cut, is_last, access.T, mortality, dense, food, land, tiles(diffusivity), tiles(drift))
    head_b, head_a = halo(head)
    head_here, dense, food = lax.optimization_barrier((head, dense, food))
    tail = start_fields(0, cut, is_last, access.T, mortality, dense, food, land)
    rate = by_row(recruit_rate)
    spawning = spawn + second + third + ring
    recruits = rate * spawning / (1.0 + spawning / 16.0)
    zero = jnp.where(rank == 0, recruits, ring) * tail[0]
    tail = lax.dynamic_update_slice(tail, zero[None], (0, 0, 0))
    tail_b, tail_a = halo(tail)

    inverse = jnp.swapaxes(zonal_inverse, 1, 2)
    rounded = lax.reduce_precision(inverse, 8, 7)
    hi, lo = rounded.astype(jnp.bfloat16), (inverse - rounded).astype(jnp.bfloat16)
    weights = jnp.concatenate(
        [jnp.concatenate([hi, lo], axis=2), jnp.concatenate([hi, jnp.zeros_like(lo)], axis=2)], axis=1
    )
    eff, strata = by_row(effort), by_row(strata_map)
    coefs = (head_b, head_here, head_a)
    out, tot1 = sweeps(4, 16 - cut, 2, cut, head_b, head_here, head_a, coefs, weights, eff, strata, None)
    out, tot0 = sweeps(4, cut, 0, 0, tail_b, tail, tail_a, coefs, weights, eff, strata, out)
    new_density = untiles(out)

    totals = jnp.sum(jnp.concatenate([tot0, tot1], axis=0), axis=2)
    length_hot = (length_bin[:, None] == jnp.arange(NLEN, dtype=jnp.int32)[None, :]).astype(jnp.float32)
    scaled = length_hot * (selectivity * (25.0 / (1024 * 4096)))[None, :]
    partial_catch = jnp.sum(totals[:, :, None] * scaled[:, None, :], axis=0).reshape(ROWS, BLK)
    table = group_sum(partial_catch, ("x", "y", "core"))
    table = group_sum(table, ("zl", "zh"))
    catch_table = table.reshape(SPAD, NLEN)[:STRATA]
    return (new_density, catch_table)


def solution(mesh):
    grid = Mesh(mesh.devices.reshape([size for _, size in AXES]), [name for name, _ in AXES])
    in_specs = (
        P(COH, LAT, None),
        P(None, LAT, None),
        P(COH, None),
        P(COH),
        P(COH),
        P(LAT, None),
        P(COH, None, None),
        P(LAT, None),
        P(LAT, None),
        P(LAT, None),
        P(LAT, None),
        P(LAT, None),
        P(COH),
        P(),
    )
    out_specs = (P(COH, LAT, None), P())
    return jax.shard_map(body, mesh=grid, in_specs=in_specs, out_specs=out_specs, check_vma=False)
```

time: 124 us -> 115 us (0.927)
  blocking collectives: 54 us -> 43.7 us
  waiting for transfers between devices: 0.02 us -> 5.75 us
  other arithmetic: 4.8 us -> 1.07 us
  local copies, waits for them, and re-layouts: 6.61 us -> 3.49 us
  Pallas kernels: 27.1 us -> 28.9 us
    all_to_all x2, blocking collectives: 54 us -> 43.7 us  [group_sum(): return jnp.sum(lax.all_to_all(copies, axes, 0, 0, tiled=True), axis=0)]
    ppermute x6 -> x4, waiting for transfers between devices: 0.02 us -> 4.01 us  [halo(): return (lax.ppermute(array, LAT, up), lax.ppermute(array, LAT, down))]
    pallas_call x1 -> x3, Pallas kernels: 5.51 us -> 9.16 us  [the longest x2 6.73 us: start_fields(): pl.pallas_call(kernel, grid=(PARTS,), in_specs=[smem, smem, smem, pl.Bloc...]
    pallas_call x3 -> x2, Pallas kernels: 21.6 us -> 19.8 us  [sweeps(): pl.pallas_call(kernel, grid=(cohorts // group,), in_specs=in_specs, out_s...]
    select_n x1 -> x0, other arithmetic: 1.64 us -> none  [body(): onward = jnp.where(rank == ranks - 1, spawn[0], spawn[1])]
    squeeze x1 -> x0, local copies, waits for them, and re-layouts: 1.57 us -> none  [body(): spawning = spawn[0] + second + third + ring]
    unnamed x17 -> x19, local copies, waits for them, and re-layouts: 3.29 us -> 2.63 us
    ppermute x6 -> x4, starting transfers between devices: 20 us -> 20.4 us  [halo(): return (lax.ppermute(array, LAT, up), lax.ppermute(array, LAT, down))]
  transfers between devices with their start and end apart: 9 -> 7, of which waited for: 0 -> 3; matrix products, arithmetic and copies ran while one was open for 8% -> 3% of each run, Pallas kernels for 16% -> 14%
where the time goes in v1:
time: 115 us; the launch traced here: 114 us
  blocking collectives  43.7 us (38%)
  starting transfers between devices  30.3 us (26%)
  Pallas kernels  28.9 us (25%)
  waiting for transfers between devices  5.75 us (5%)
  local copies, waits for them, and re-layouts  3.49 us (3%)
    all_to_all x2, blocking collectives, group_sum(): return jnp.sum(lax.all_to_all(copies, axes, 0, 0, tiled=True), axis=0)  43.7 us
    ppermute x4, starting transfers between devices, halo(): return (lax.ppermute(array, LAT, up), lax.ppermute(array, LAT, down))  20.4 us
    pallas_call x2, Pallas kernels, sweeps(): pl.pallas_call(kernel, grid=(cohorts // group,), in_specs=in_specs, out_s...  19.8 us
    ppermute x1, starting transfers between devices, body(): ring = lax.ppermute(onward, COH, [(k, (k + 1) % 4) for k in range(4)])  7.28 us
    pallas_call x2, Pallas kernels, start_fields(): pl.pallas_call(kernel, grid=(PARTS,), in_specs=[smem, smem, smem, pl.Bloc...  6.73 us
    ppermute x4, waiting for transfers between devices, halo(): return (lax.ppermute(array, LAT, up), lax.ppermute(array, LAT, down))  4.01 us
    unnamed x19, local copies, waits for them, and re-layouts  2.63 us
    pallas_call x1, Pallas kernels, local_spawn(): pl.pallas_call(spawn_kernel, grid=(PARTS,), in_specs=[smem, smem, pl.Bloc...  2.43 us
  transfers between devices with their start and end apart: 7, of which 3 were waited for; matrix products, arithmetic and copies ran while one was open for 3% of the time, Pallas kernels for 14%

profile of v1, /device:TPU:1, one launch (start us, length us, event | category | flops | bytes accessed | tf_op | source)
XLA Modules:
  0.0 114.1 jit_solution(8943743860257273535)
XLA Ops:
  0.6 3.4 %start_fields.2.refs_1_.refs_4_ = f32[10,256,128]{2,1,0:T(8,128)} custom-call(f32[1]{0:T(128)} %bitcast.refs_0_.flag, f32[6,16]{1,0:T(8,128)} %bitcast.58, f32[16]{0:T(128)} %refs_2_.3, f32[16,256,128]{2,1,0:T(8,128)} %bitcast.48, f32[6,256,128]{2,1,0:T(8,128)} %bitcast.51, s32[256,128]{1,0:T(8,128)} %bitcast.53, f32[256,128]{1,0:T(8,128)} %bitcast.55, ...), custom_call_target="tpu_custom_call" | custom-call | flops 5242880 | bytes 4194304 | tf_op jit(solution)/shard_map/start_fields/pallas_call | solution.py:99
  4.1 0.0 copy-start.6
  4.1 4.7 %collective-permute-start.5 = (f32[10,256,128]{2,1,0:T(8,128)}, f32[10,256,128]{2,1,0:T(8,128)S(1)}, u32[]{:S(2)}, u32[]{:S(2)}) collective-permute-start(f32[10,256,128]{2,1,0:T(8,128)} %start_fields.2.refs_1_.refs_4_), channel_id=1, source_target_pairs={{0,4},{4,8},{8,12},{12,16},{16,20},{20,24},{24,28},{28,32},{32,36}... | collective-permute-start | bytes 3932168 | tf_op jit(solution)/shard_map/ppermute | solution.py:287
  8.8 5.6 %collective-permute-start.6 = (f32[10,256,128]{2,1,0:T(8,128)}, f32[10,256,128]{2,1,0:T(8,128)S(1)}, u32[]{:S(2)}, u32[]{:S(2)}) collective-permute-start(f32[10,256,128]{2,1,0:T(8,128)} %start_fields.2.refs_1_.refs_4_), channel_id=1, source_target_pairs={{4,0},{8,4},{12,8},{16,12},{20,16},{24,20},{28,24},{32,28},{36,32}... | collective-permute-start | bytes 3932168 | tf_op jit(solution)/shard_map/ppermute | solution.py:287
  14.4 2.4 %local_spawn.1 = (f32[256,128]{1,0:T(8,128)}, f32[256,128]{1,0:T(8,128)}) custom-call(f32[1]{0:T(128)} %bitcast.refs_0_.flag, f32[16]{0:T(128)} %maturity.1, f32[16,256,128]{2,1,0:T(8,128)} %bitcast.49), custom_call_target="tpu_custom_call" | custom-call | flops 1048576 | bytes 3145728 | tf_op jit(solution)/shard_map/local_spawn/pallas_call | solution.py:47
  16.8 1.3 %collective-permute-start = (f32[256,128]{1,0:T(8,128)}, f32[256,128]{1,0:T(8,128)S(1)}, u32[]{:S(2)}, u32[]{:S(2)}) collective-permute-start(f32[256,128]{1,0:T(8,128)} %get-tuple-element.13), channel_id=1, source_target_pairs={{1,0},{5,4},{9,8},{13,12},{17,16},{21,20},{25,24},{29,28},{33,32},... | collective-permute-start | bytes 393224 | tf_op jit(solution)/shard_map/ppermute | solution.py:294
  18.1 1.3 %collective-permute-start.1 = (f32[256,128]{1,0:T(8,128)}, f32[256,128]{1,0:T(8,128)S(1)}, u32[]{:S(2)}, u32[]{:S(2)}) collective-permute-start(f32[256,128]{1,0:T(8,128)} %get-tuple-element.13), channel_id=1, source_target_pairs={{2,0},{6,4},{10,8},{14,12},{18,16},{22,20},{26,24},{30,28},{34,32}... | collective-permute-start | bytes 393224 | tf_op jit(solution)/shard_map/ppermute | solution.py:295
  19.4 7.3 %collective-permute-start.2 = (f32[256,128]{1,0:T(8,128)}, f32[256,128]{1,0:T(8,128)S(1)}, u32[]{:S(2)}, u32[]{:S(2)}) collective-permute-start(f32[256,128]{1,0:T(8,128)} %get-tuple-element.14), channel_id=1, source_target_pairs={{0,1},{1,2},{2,3},{3,0},{4,5},{5,6},{6,7},{7,4},{8,9},{9,10},{10,1... | collective-permute-start | bytes 393224 | tf_op jit(solution)/shard_map/ppermute | solution.py:293
  26.8 2.6 %copy.18 = f32[16,128,128]{1,2,0:T(8,128)} copy(f32[16,128,128]{2,1,0:T(8,128)} %param.20) | data formatting | bytes 2097152 | tf_op args[6]
  29.4 0.0 copy-start.8
  29.5 3.3 %start_fields.3 = f32[8,256,128]{2,1,0:T(8,128)} custom-call(f32[1]{0:T(128)} %bitcast.refs_0_.flag, f32[6,16]{1,0:T(8,128)} %bitcast.59, f32[16]{0:T(128)} %refs_2_.3, f32[16,256,128]{2,1,0:T(8,128)} %bitcast.50, f32[6,256,128]{2,1,0:T(8,128)} %bitcast.52, s32[256,128]{1,0:T(8,128)} %bitcast.54), custom_call_target="tpu_custom_call" | custom-call | flops 5242880 | bytes 4194304 | tf_op jit(solution)/shard_map/start_fields/pallas_call | solution.py:99
  32.8 0.3 fusion.2
  33.0 0.0 copy-start.7
  33.1 0.0 copy-start.1
  33.1 0.3 fusion.1.refs_6_
  33.4 0.0 collective-permute-done
  33.4 1.1 collective-permute-done.1
  34.5 0.6 collective-permute-done.2
  35.2 0.1 fusion.5.refs_1_
  35.2 8.0 %collective-permute-start.3 = (f32[8,256,128]{2,1,0:T(8,128)S(1)}, f32[8,256,128]{2,1,0:T(8,128)S(1)}, u32[]{:S(2)}, u32[]{:S(2)}) collective-permute-start(f32[8,256,128]{2,1,0:T(8,128)S(1)} %fusion.5.refs_1_), channel_id=1, source_target_pairs={{0,4},{4,8},{8,12},{12,16},{16,20},{20,24},{24,28},{28,32},{32,36}... | collective-permute-start | bytes 3145736 | tf_op jit(solution)/shard_map/ppermute | solution.py:287
  43.3 2.1 %collective-permute-start.4 = (f32[8,256,128]{2,1,0:T(8,128)S(1)}, f32[8,256,128]{2,1,0:T(8,128)S(1)}, u32[]{:S(2)}, u32[]{:S(2)}) collective-permute-start(f32[8,256,128]{2,1,0:T(8,128)S(1)} %fusion.5.refs_1_), channel_id=1, source_target_pairs={{4,0},{8,4},{12,8},{16,12},{20,16},{24,20},{28,24},{32,28},{36,32}... | collective-permute-start | bytes 3145736 | tf_op jit(solution)/shard_map/ppermute | solution.py:287
  45.4 0.1 fusion.6
  45.5 0.0 collective-permute-done.5.refs_0_.refs_3_
  45.5 9.9 %sweeps.2 = (f32[16,256,128]{2,1,0:T(8,128)}, f32[8,32,128]{2,1,0:T(8,128)S(1)}) custom-call(f32[10,256,128]{2,1,0:T(8,128)S(1)} %collective-permute-done.5.refs_0_.refs_3_, f32[10,256,128]{2,1,0:T(8,128)S(1)} %copy-done.1, f32[10,256,128]{2,1,0:T(8,128)S(1)} %collective-permute-done.6.refs_2_.refs_5_, ...), custom_call_target="tpu_custom_call" | custom-call | flops 8800000000 | bytes 33554432 | tf_op jit(solution)/shard_map/sweeps/pallas_call | solution.py:221
  55.4 4.0 %collective-permute-done.4.refs_2_ = f32[8,256,128]{2,1,0:T(8,128)S(1)} collective-permute-done((f32[8,256,128]{2,1,0:T(8,128)S(1)}, f32[8,256,128]{2,1,0:T(8,128)S(1)}, u32[]{:S(2)}, u32[]{:S(2)}) %collective-permute-start.4) | collective-permute-done | bytes 1048608 | tf_op jit(solution)/shard_map/ppermute | solution.py:287
  59.4 9.9 %sweeps.3 = (f32[16,256,128]{2,1,0:T(8,128)}, f32[8,32,128]{2,1,0:T(8,128)S(1)}) custom-call(f32[8,256,128]{2,1,0:T(8,128)S(1)} %collective-permute-done.3.refs_0_, f32[8,256,128]{2,1,0:T(8,128)S(1)} %fusion.5.refs_1_, f32[8,256,128]{2,1,0:T(8,128)S(1)} %collective-permute-done.4.refs_2_, ...), custom_call_target="tpu_custom_call", output_to_operand_aliasing={{0}: (9, {})} | custom-call | flops 8800000000 | bytes 33554432 | tf_op jit(solution)/shard_map/sweeps/pallas_call | solution.py:221
  69.3 0.1 maximum_reduce_fusion
  69.4 0.1 multiply_reduce_fusion
  69.5 0.1 broadcast_in_dim.9
  69.6 29.6 %all_to_all.10 = f32[32,8,128]{2,1,0:T(8,128)S(1)} all-to-all(f32[32,8,128]{2,1,0:T(8,128)S(1)} %broadcast_in_dim.10), channel_id=1, replica_groups=mesh['zl'=4,'x'=4,'y'=4,'core'=2,'zh'=4] {'x','y','core'}, dimensions={0} | all-to-all | bytes 262144 | tf_op jit(solution)/shard_map/all_to_all | solution.py:261
  99.3 14.1 %all_to_all.11 = f32[16,8,128]{2,1,0:T(8,128)S(1)} all-to-all(f32[16,8,128]{2,1,0:T(8,128)S(1)} %broadcast_in_dim.11), channel_id=1, replica_groups=mesh['zl'=4,'x'=4,'y'=4,'core'=2,'zh'=4] {'zl','zh'}, dimensions={0} | all-to-all | bytes 131072 | tf_op jit(solution)/shard_map/all_to_all | solution.py:261
  113.4 0.7 reshape.103
  (24 shorter events, 0.2 us)
Async XLA Ops:
  4.1 22.6 %copy-start.4 = (f32[8,4096]{1,0:T(8,128)S(1)}, f32[8,4096]{1,0:T(8,128)}, u32[]{:S(2)}) copy-start(f32[8,4096]{1,0:T(8,128)} %param.19) | copy-start | bytes 393220
  4.1 25.3 %copy-start.5 = (s32[8,4096]{1,0:T(8,128)S(1)}, s32[8,4096]{1,0:T(8,128)}, u32[]{:S(2)}) copy-start(s32[8,4096]{1,0:T(8,128)} %param.25) | copy-start | bytes 393220
  4.1 25.3 %copy-start.6 = (f32[8,4096]{1,0:T(8,128)S(1)}, f32[8,4096]{1,0:T(8,128)}, u32[]{:S(2)}) copy-start(f32[8,4096]{1,0:T(8,128)} %param.24) | copy-start | bytes 393220
  4.1 41.4 %collective-permute-start.5 = (f32[10,256,128]{2,1,0:T(8,128)}, f32[10,256,128]{2,1,0:T(8,128)S(1)}, u32[]{:S(2)}, u32[]{:S(2)}) collective-permute-start(f32[10,256,128]{2,1,0:T(8,128)} %start_fields.2.refs_1_.refs_4_), channel_id=1, source_target_pairs={{0,4},{4,8},{8,12},{12,16},{16,20},{20,24},{24,28},{28,32},{32,36}... | collective-permute-start | bytes 3932168 | tf_op jit(solution)/shard_map/ppermute | solution.py:287
  8.8 36.6 %collective-permute-start.6 = (f32[10,256,128]{2,1,0:T(8,128)}, f32[10,256,128]{2,1,0:T(8,128)S(1)}, u32[]{:S(2)}, u32[]{:S(2)}) collective-permute-start(f32[10,256,128]{2,1,0:T(8,128)} %start_fields.2.refs_1_.refs_4_), channel_id=1, source_target_pairs={{4,0},{8,4},{12,8},{16,12},{20,16},{24,20},{28,24},{32,28},{36,32}... | collective-permute-start | bytes 3932168 | tf_op jit(solution)/shard_map/ppermute | solution.py:287
  16.8 16.6 %collective-permute-start = (f32[256,128]{1,0:T(8,128)}, f32[256,128]{1,0:T(8,128)S(1)}, u32[]{:S(2)}, u32[]{:S(2)}) collective-permute-start(f32[256,128]{1,0:T(8,128)} %get-tuple-element.13), channel_id=1, source_target_pairs={{1,0},{5,4},{9,8},{13,12},{17,16},{21,20},{25,24},{29,28},{33,32},... | collective-permute-start | bytes 393224 | tf_op jit(solution)/shard_map/ppermute | solution.py:294
  18.1 16.4 %collective-permute-start.1 = (f32[256,128]{1,0:T(8,128)}, f32[256,128]{1,0:T(8,128)S(1)}, u32[]{:S(2)}, u32[]{:S(2)}) collective-permute-start(f32[256,128]{1,0:T(8,128)} %get-tuple-element.13), channel_id=1, source_target_pairs={{2,0},{6,4},{10,8},{14,12},{18,16},{22,20},{26,24},{30,28},{34,32}... | collective-permute-start | bytes 393224 | tf_op jit(solution)/shard_map/ppermute | solution.py:295
  19.4 15.7 %collective-permute-start.2 = (f32[256,128]{1,0:T(8,128)}, f32[256,128]{1,0:T(8,128)S(1)}, u32[]{:S(2)}, u32[]{:S(2)}) collective-permute-start(f32[256,128]{1,0:T(8,128)} %get-tuple-element.14), channel_id=1, source_target_pairs={{0,1},{1,2},{2,3},{3,0},{4,5},{5,6},{6,7},{7,4},{8,9},{9,10},{10,1... | collective-permute-start | bytes 393224 | tf_op jit(solution)/shard_map/ppermute | solution.py:293
  29.4 3.3 %copy-start.8 = (f32[32]{0:T(128)S(1)}, f32[32]{0:T(128)}, u32[]{:S(2)}) copy-start(f32[32]{0:T(128)} %param.27) | copy-start | bytes 388
  29.4 3.3 %copy-start.2 = (f32[16,128,128]{1,2,0:T(8,128)S(1)}, f32[16,128,128]{1,2,0:T(8,128)}, u32[]{:S(2)}) copy-start(f32[16,128,128]{1,2,0:T(8,128)} %copy.18) | copy-start | bytes 3145732
  33.0 2.1 %copy-start = (f32[8,256,128]{2,1,0:T(8,128)S(1)}, f32[8,256,128]{2,1,0:T(8,128)}, u32[]{:S(2)}) copy-start(f32[8,256,128]{2,1,0:T(8,128)} %start_fields.3) | copy-start | bytes 3145732
  33.0 2.1 %copy-start.3 = (f32[256,128]{1,0:T(8,128)S(1)}, f32[256,128]{1,0:T(8,128)}, u32[]{:S(2)}) copy-start(f32[256,128]{1,0:T(8,128)} %get-tuple-element.13) | copy-start | bytes 393220
  33.0 12.4 %copy-start.7 = (s32[16]{0:T(128)S(1)}, s32[16]{0:T(128)}, u32[]{:S(2)}) copy-start(s32[16]{0:T(128)} %param.26) | copy-start | bytes 196
  33.1 12.4 %copy-start.1 = (f32[10,256,128]{2,1,0:T(8,128)S(1)}, f32[10,256,128]{2,1,0:T(8,128)}, u32[]{:S(2)}) copy-start(f32[10,256,128]{2,1,0:T(8,128)} %start_fields.2.refs_1_.refs_4_) | copy-start | bytes 3932164
  35.2 20.2 %collective-permute-start.3 = (f32[8,256,128]{2,1,0:T(8,128)S(1)}, f32[8,256,128]{2,1,0:T(8,128)S(1)}, u32[]{:S(2)}, u32[]{:S(2)}) collective-permute-start(f32[8,256,128]{2,1,0:T(8,128)S(1)} %fusion.5.refs_1_), channel_id=1, source_target_pairs={{0,4},{4,8},{8,12},{12,16},{16,20},{20,24},{24,28},{28,32},{32,36}... | collective-permute-start | bytes 3145736 | tf_op jit(solution)/shard_map/ppermute | solution.py:287
  43.3 16.1 %collective-permute-start.4 = (f32[8,256,128]{2,1,0:T(8,128)S(1)}, f32[8,256,128]{2,1,0:T(8,128)S(1)}, u32[]{:S(2)}, u32[]{:S(2)}) collective-permute-start(f32[8,256,128]{2,1,0:T(8,128)S(1)} %fusion.5.refs_1_), channel_id=1, source_target_pairs={{4,0},{8,4},{12,8},{16,12},{20,16},{24,20},{28,24},{32,28},{36,32}... | collective-permute-start | bytes 3145736 | tf_op jit(solution)/shard_map/ppermute | solution.py:287

commit v2 on v1

--- a/solution.py
+++ b/solution.py
@@ -56,10 +56,10 @@
     )(flag, maturity, density)
 
 
-def start_kernel(first, count, flag, access, mortality, density, forage, land, *refs):
+def start_kernel(first, count, flag, access, mortality, before, density, forage, land, *refs):
     part = pl.program_id(0)
     groups = forage.shape[0]
-    last = density.shape[0] - 1
+    last = access.shape[1] - 1
     out = refs[-1]
     lead = out.shape[0] - count
     for t in range(0, PART // ROWS, STEP):
@@ -81,9 +81,9 @@
                     total = total + weights[g] * food[g][i]
                 gain = decay * ocean[i] * (1.0 + 0.5 * jnp.tanh(total))
                 if c > 0:
-                    aged = density[c - 1, at, :]
+                    aged = before[0, at, :] if j == 0 else density[j - 1, at, :]
                     if c == last:
-                        aged = aged + flag[0] * density[last, at, :]
+                        aged = aged + flag[0] * density[j, at, :]
                     gain = aged * gain
                 out[lead + j, rows[i], :] = gain
 
@@ -103,7 +103,8 @@
             smem,
             smem,
             smem,
-            pl.BlockSpec((density.shape[0], PART, BLK), lambda p: (0, p, 0)),
+            pl.BlockSpec((1, PART, BLK), lambda p: (max(first - 1, 0), p, 0)),
+            pl.BlockSpec((count, PART, BLK), lambda p: (first // count, p, 0)),
             pl.BlockSpec((forage.shape[0], PART, BLK), lambda p: (0, p, 0)),
         ]
         + [flat] * (1 + len(coefficients)),
@@ -112,7 +113,7 @@
         compiler_params=pltpu.CompilerParams(vmem_limit_bytes=VMEM),
         cost_estimate=pl.CostEstimate(flops=20 * count * BAND * BLK, bytes_accessed=4 * 1024 * 1024, transcendentals=count * BAND * BLK),
         name="start_fields",
-    )(flag, access, mortality, density, forage, land, *coefficients)
+    )(flag, access, mortality, density, density, forage, land, *coefficients)
 
 
 def sweep_kernel(group, before, own, after, coef_b, coef_o, coef_a, weights, effort, strata, filled, out, totals, c0, cn, cs, *scratch):

time: 115 us -> 114 us (level)
  no operation moved by 1% of the time
where the time goes in v2:
time: 114 us
  blocking collectives  43.7 us (38%)
  starting transfers between devices  30.3 us (27%)
  Pallas kernels  28.7 us (25%)
  waiting for transfers between devices  5.88 us (5%)
  local copies, waits for them, and re-layouts  3.49 us (3%)
    all_to_all x2, blocking collectives, group_sum(): return jnp.sum(lax.all_to_all(copies, axes, 0, 0, tiled=True), axis=0)  43.7 us
    ppermute x4, starting transfers between devices, halo(): return (lax.ppermute(array, LAT, up), lax.ppermute(array, LAT, down))  20.4 us
    pallas_call x2, Pallas kernels, sweeps(): pl.pallas_call(kernel, grid=(cohorts // group,), in_specs=in_specs, out_s...  19.8 us
    ppermute x1, starting transfers between devices, body(): ring = lax.ppermute(onward, COH, [(k, (k + 1) % 4) for k in range(4)])  7.28 us
    pallas_call x2, Pallas kernels, start_fields(): pl.pallas_call(kernel, grid=(PARTS,), in_specs=[smem, smem, smem, pl.Bloc...  6.5 us
    ppermute x4, waiting for transfers between devices, halo(): return (lax.ppermute(array, LAT, up), lax.ppermute(array, LAT, down))  4 us
    unnamed x19, local copies, waits for them, and re-layouts  2.63 us
    pallas_call x1, Pallas kernels, local_spawn(): pl.pallas_call(spawn_kernel, grid=(PARTS,), in_specs=[smem, smem, pl.Bloc...  2.43 us
  transfers between devices with their start and end apart: 7, of which 3 were waited for; matrix products, arithmetic and copies ran while one was open for 3% of the time, Pallas kernels for 14%

profile of v2, /device:TPU:1, one launch (start us, length us, event | category | flops | bytes accessed | tf_op | source)
XLA Modules:
  0.0 114.0 jit_solution(665669813242142530)
XLA Ops:
  0.6 3.3 %start_fields.2.refs_1_.refs_4_ = f32[10,256,128]{2,1,0:T(8,128)} custom-call(f32[1]{0:T(128)} %bitcast.refs_0_.flag, f32[6,16]{1,0:T(8,128)} %bitcast.60, f32[16]{0:T(128)} %refs_2_.3, f32[16,256,128]{2,1,0:T(8,128)} %bitcast.48, f32[16,256,128]{2,1,0:T(8,128)} %bitcast.49, f32[6,256,128]{2,1,0:T(8,128)} %bitcast.53, s32[256,128]{1,0:T(8,128)} %bitcast.55, ...), custom_call_target="tpu_custom_call" | custom-call | flops 5242880 | bytes 4194304 | tf_op jit(solution)/shard_map/start_fields/pallas_call | solution.py:99
  4.0 0.0 copy-start.6
  4.0 4.7 %collective-permute-start.5 = (f32[10,256,128]{2,1,0:T(8,128)}, f32[10,256,128]{2,1,0:T(8,128)S(1)}, u32[]{:S(2)}, u32[]{:S(2)}) collective-permute-start(f32[10,256,128]{2,1,0:T(8,128)} %start_fields.2.refs_1_.refs_4_), channel_id=1, source_target_pairs={{0,4},{4,8},{8,12},{12,16},{16,20},{20,24},{24,28},{28,32},{32,36}... | collective-permute-start | bytes 3932168 | tf_op jit(solution)/shard_map/ppermute | solution.py:288
  8.7 5.6 %collective-permute-start.6 = (f32[10,256,128]{2,1,0:T(8,128)}, f32[10,256,128]{2,1,0:T(8,128)S(1)}, u32[]{:S(2)}, u32[]{:S(2)}) collective-permute-start(f32[10,256,128]{2,1,0:T(8,128)} %start_fields.2.refs_1_.refs_4_), channel_id=1, source_target_pairs={{4,0},{8,4},{12,8},{16,12},{20,16},{24,20},{28,24},{32,28},{36,32}... | collective-permute-start | bytes 3932168 | tf_op jit(solution)/shard_map/ppermute | solution.py:288
  14.3 2.4 %local_spawn.1 = (f32[256,128]{1,0:T(8,128)}, f32[256,128]{1,0:T(8,128)}) custom-call(f32[1]{0:T(128)} %bitcast.refs_0_.flag, f32[16]{0:T(128)} %maturity.1, f32[16,256,128]{2,1,0:T(8,128)} %bitcast.50), custom_call_target="tpu_custom_call" | custom-call | flops 1048576 | bytes 3145728 | tf_op jit(solution)/shard_map/local_spawn/pallas_call | solution.py:47
  16.7 1.3 %collective-permute-start = (f32[256,128]{1,0:T(8,128)}, f32[256,128]{1,0:T(8,128)S(1)}, u32[]{:S(2)}, u32[]{:S(2)}) collective-permute-start(f32[256,128]{1,0:T(8,128)} %get-tuple-element.13), channel_id=1, source_target_pairs={{1,0},{5,4},{9,8},{13,12},{17,16},{21,20},{25,24},{29,28},{33,32},... | collective-permute-start | bytes 393224 | tf_op jit(solution)/shard_map/ppermute | solution.py:295
  18.0 1.3 %collective-permute-start.1 = (f32[256,128]{1,0:T(8,128)}, f32[256,128]{1,0:T(8,128)S(1)}, u32[]{:S(2)}, u32[]{:S(2)}) collective-permute-start(f32[256,128]{1,0:T(8,128)} %get-tuple-element.13), channel_id=1, source_target_pairs={{2,0},{6,4},{10,8},{14,12},{18,16},{22,20},{26,24},{30,28},{34,32}... | collective-permute-start | bytes 393224 | tf_op jit(solution)/shard_map/ppermute | solution.py:296
  19.3 7.3 %collective-permute-start.2 = (f32[256,128]{1,0:T(8,128)}, f32[256,128]{1,0:T(8,128)S(1)}, u32[]{:S(2)}, u32[]{:S(2)}) collective-permute-start(f32[256,128]{1,0:T(8,128)} %get-tuple-element.14), channel_id=1, source_target_pairs={{0,1},{1,2},{2,3},{3,0},{4,5},{5,6},{6,7},{7,4},{8,9},{9,10},{10,1... | collective-permute-start | bytes 393224 | tf_op jit(solution)/shard_map/ppermute | solution.py:294
  26.7 2.6 %copy.18 = f32[16,128,128]{1,2,0:T(8,128)} copy(f32[16,128,128]{2,1,0:T(8,128)} %param.20) | data formatting | bytes 2097152 | tf_op args[6]
  29.3 0.0 copy-start.8
  29.4 3.2 %start_fields.3 = f32[8,256,128]{2,1,0:T(8,128)} custom-call(f32[1]{0:T(128)} %bitcast.refs_0_.flag, f32[6,16]{1,0:T(8,128)} %bitcast.61, f32[16]{0:T(128)} %refs_2_.3, f32[16,256,128]{2,1,0:T(8,128)} %bitcast.51, f32[16,256,128]{2,1,0:T(8,128)} %bitcast.52, f32[6,256,128]{2,1,0:T(8,128)} %bitcast.54, s32[256,128]{1,0:T(8,128)} %bitcast.56), custom_call_target="tpu_custom_call" | custom-call | flops 5242880 | bytes 4194304 | tf_op jit(solution)/shard_map/start_fields/pallas_call | solution.py:99
  32.5 0.3 fusion.2
  32.8 0.0 copy-start.7
  32.8 0.0 copy-start.1
  32.8 0.3 fusion.1.refs_6_
  33.2 0.0 collective-permute-done
  33.2 1.2 %collective-permute-done.1 = f32[256,128]{1,0:T(8,128)S(1)} collective-permute-done((f32[256,128]{1,0:T(8,128)}, f32[256,128]{1,0:T(8,128)S(1)}, u32[]{:S(2)}, u32[]{:S(2)}) %collective-permute-start.1) | collective-permute-done | bytes 131104 | tf_op jit(solution)/shard_map/ppermute | solution.py:296
  34.4 0.6 collective-permute-done.2
  35.1 0.1 fusion.5.refs_1_
  35.1 8.0 %collective-permute-start.3 = (f32[8,256,128]{2,1,0:T(8,128)S(1)}, f32[8,256,128]{2,1,0:T(8,128)S(1)}, u32[]{:S(2)}, u32[]{:S(2)}) collective-permute-start(f32[8,256,128]{2,1,0:T(8,128)S(1)} %fusion.5.refs_1_), channel_id=1, source_target_pairs={{0,4},{4,8},{8,12},{12,16},{16,20},{20,24},{24,28},{28,32},{32,36}... | collective-permute-start | bytes 3145736 | tf_op jit(solution)/shard_map/ppermute | solution.py:288
  43.2 2.1 %collective-permute-start.4 = (f32[8,256,128]{2,1,0:T(8,128)S(1)}, f32[8,256,128]{2,1,0:T(8,128)S(1)}, u32[]{:S(2)}, u32[]{:S(2)}) collective-permute-start(f32[8,256,128]{2,1,0:T(8,128)S(1)} %fusion.5.refs_1_), channel_id=1, source_target_pairs={{4,0},{8,4},{12,8},{16,12},{20,16},{24,20},{28,24},{32,28},{36,32}... | collective-permute-start | bytes 3145736 | tf_op jit(solution)/shard_map/ppermute | solution.py:288
  45.3 0.1 fusion.6
  45.4 9.9 %sweeps.2 = (f32[16,256,128]{2,1,0:T(8,128)}, f32[8,32,128]{2,1,0:T(8,128)S(1)}) custom-call(f32[10,256,128]{2,1,0:T(8,128)S(1)} %collective-permute-done.5.refs_0_.refs_3_, f32[10,256,128]{2,1,0:T(8,128)S(1)} %copy-done.1, f32[10,256,128]{2,1,0:T(8,128)S(1)} %collective-permute-done.6.refs_2_.refs_5_, ...), custom_call_target="tpu_custom_call" | custom-call | flops 8800000000 | bytes 33554432 | tf_op jit(solution)/shard_map/sweeps/pallas_call | solution.py:222
  55.3 0.0 collective-permute-done.3.refs_0_
  55.3 4.0 %collective-permute-done.4.refs_2_ = f32[8,256,128]{2,1,0:T(8,128)S(1)} collective-permute-done((f32[8,256,128]{2,1,0:T(8,128)S(1)}, f32[8,256,128]{2,1,0:T(8,128)S(1)}, u32[]{:S(2)}, u32[]{:S(2)}) %collective-permute-start.4) | collective-permute-done | bytes 1048608 | tf_op jit(solution)/shard_map/ppermute | solution.py:288
  59.3 9.9 %sweeps.3 = (f32[16,256,128]{2,1,0:T(8,128)}, f32[8,32,128]{2,1,0:T(8,128)S(1)}) custom-call(f32[8,256,128]{2,1,0:T(8,128)S(1)} %collective-permute-done.3.refs_0_, f32[8,256,128]{2,1,0:T(8,128)S(1)} %fusion.5.refs_1_, f32[8,256,128]{2,1,0:T(8,128)S(1)} %collective-permute-done.4.refs_2_, ...), custom_call_target="tpu_custom_call", output_to_operand_aliasing={{0}: (9, {})} | custom-call | flops 8800000000 | bytes 33554432 | tf_op jit(solution)/shard_map/sweeps/pallas_call | solution.py:222
  69.2 0.1 maximum_reduce_fusion
  69.3 0.1 multiply_reduce_fusion
  69.4 0.1 broadcast_in_dim.9
  69.5 29.6 %all_to_all.10 = f32[32,8,128]{2,1,0:T(8,128)S(1)} all-to-all(f32[32,8,128]{2,1,0:T(8,128)S(1)} %broadcast_in_dim.10), channel_id=1, replica_groups=mesh['zl'=4,'x'=4,'y'=4,'core'=2,'zh'=4] {'x','y','core'}, dimensions={0} | all-to-all | bytes 262144 | tf_op jit(solution)/shard_map/all_to_all | solution.py:262
  99.2 14.1 %all_to_all.11 = f32[16,8,128]{2,1,0:T(8,128)S(1)} all-to-all(f32[16,8,128]{2,1,0:T(8,128)S(1)} %broadcast_in_dim.11), channel_id=1, replica_groups=mesh['zl'=4,'x'=4,'y'=4,'core'=2,'zh'=4] {'zl','zh'}, dimensions={0} | all-to-all | bytes 131072 | tf_op jit(solution)/shard_map/all_to_all | solution.py:262
  113.3 0.7 reshape.103
  (24 shorter events, 0.2 us)
Async XLA Ops:
  4.0 22.6 %copy-start.4 = (f32[8,4096]{1,0:T(8,128)S(1)}, f32[8,4096]{1,0:T(8,128)}, u32[]{:S(2)}) copy-start(f32[8,4096]{1,0:T(8,128)} %param.19) | copy-start | bytes 393220
  4.0 25.3 %copy-start.5 = (s32[8,4096]{1,0:T(8,128)S(1)}, s32[8,4096]{1,0:T(8,128)}, u32[]{:S(2)}) copy-start(s32[8,4096]{1,0:T(8,128)} %param.25) | copy-start | bytes 393220
  4.0 25.3 %copy-start.6 = (f32[8,4096]{1,0:T(8,128)S(1)}, f32[8,4096]{1,0:T(8,128)}, u32[]{:S(2)}) copy-start(f32[8,4096]{1,0:T(8,128)} %param.24) | copy-start | bytes 393220
  4.0 41.4 %collective-permute-start.5 = (f32[10,256,128]{2,1,0:T(8,128)}, f32[10,256,128]{2,1,0:T(8,128)S(1)}, u32[]{:S(2)}, u32[]{:S(2)}) collective-permute-start(f32[10,256,128]{2,1,0:T(8,128)} %start_fields.2.refs_1_.refs_4_), channel_id=1, source_target_pairs={{0,4},{4,8},{8,12},{12,16},{16,20},{20,24},{24,28},{28,32},{32,36}... | collective-permute-start | bytes 3932168 | tf_op jit(solution)/shard_map/ppermute | solution.py:288
  8.7 36.6 %collective-permute-start.6 = (f32[10,256,128]{2,1,0:T(8,128)}, f32[10,256,128]{2,1,0:T(8,128)S(1)}, u32[]{:S(2)}, u32[]{:S(2)}) collective-permute-start(f32[10,256,128]{2,1,0:T(8,128)} %start_fields.2.refs_1_.refs_4_), channel_id=1, source_target_pairs={{4,0},{8,4},{12,8},{16,12},{20,16},{24,20},{28,24},{32,28},{36,32}... | collective-permute-start | bytes 3932168 | tf_op jit(solution)/shard_map/ppermute | solution.py:288
  16.7 16.4 %collective-permute-start = (f32[256,128]{1,0:T(8,128)}, f32[256,128]{1,0:T(8,128)S(1)}, u32[]{:S(2)}, u32[]{:S(2)}) collective-permute-start(f32[256,128]{1,0:T(8,128)} %get-tuple-element.13), channel_id=1, source_target_pairs={{1,0},{5,4},{9,8},{13,12},{17,16},{21,20},{25,24},{29,28},{33,32},... | collective-permute-start | bytes 393224 | tf_op jit(solution)/shard_map/ppermute | solution.py:295
  18.0 16.4 %collective-permute-start.1 = (f32[256,128]{1,0:T(8,128)}, f32[256,128]{1,0:T(8,128)S(1)}, u32[]{:S(2)}, u32[]{:S(2)}) collective-permute-start(f32[256,128]{1,0:T(8,128)} %get-tuple-element.13), channel_id=1, source_target_pairs={{2,0},{6,4},{10,8},{14,12},{18,16},{22,20},{26,24},{30,28},{34,32}... | collective-permute-start | bytes 393224 | tf_op jit(solution)/shard_map/ppermute | solution.py:296
  19.3 15.7 %collective-permute-start.2 = (f32[256,128]{1,0:T(8,128)}, f32[256,128]{1,0:T(8,128)S(1)}, u32[]{:S(2)}, u32[]{:S(2)}) collective-permute-start(f32[256,128]{1,0:T(8,128)} %get-tuple-element.14), channel_id=1, source_target_pairs={{0,1},{1,2},{2,3},{3,0},{4,5},{5,6},{6,7},{7,4},{8,9},{9,10},{10,1... | collective-permute-start | bytes 393224 | tf_op jit(solution)/shard_map/ppermute | solution.py:294
  29.3 3.2 %copy-start.8 = (f32[32]{0:T(128)S(1)}, f32[32]{0:T(128)}, u32[]{:S(2)}) copy-start(f32[32]{0:T(128)} %param.27) | copy-start | bytes 388
  29.3 3.2 %copy-start.2 = (f32[16,128,128]{1,2,0:T(8,128)S(1)}, f32[16,128,128]{1,2,0:T(8,128)}, u32[]{:S(2)}) copy-start(f32[16,128,128]{1,2,0:T(8,128)} %copy.18) | copy-start | bytes 3145732
  32.8 2.3 %copy-start = (f32[8,256,128]{2,1,0:T(8,128)S(1)}, f32[8,256,128]{2,1,0:T(8,128)}, u32[]{:S(2)}) copy-start(f32[8,256,128]{2,1,0:T(8,128)} %start_fields.3) | copy-start | bytes 3145732
  32.8 2.2 %copy-start.3 = (f32[256,128]{1,0:T(8,128)S(1)}, f32[256,128]{1,0:T(8,128)}, u32[]{:S(2)}) copy-start(f32[256,128]{1,0:T(8,128)} %get-tuple-element.13) | copy-start | bytes 393220
  32.8 12.5 %copy-start.7 = (s32[16]{0:T(128)S(1)}, s32[16]{0:T(128)}, u32[]{:S(2)}) copy-start(s32[16]{0:T(128)} %param.26) | copy-start | bytes 196
  32.8 12.6 %copy-start.1 = (f32[10,256,128]{2,1,0:T(8,128)S(1)}, f32[10,256,128]{2,1,0:T(8,128)}, u32[]{:S(2)}) copy-start(f32[10,256,128]{2,1,0:T(8,128)} %start_fields.2.refs_1_.refs_4_) | copy-start | bytes 3932164
  35.1 20.2 %collective-permute-start.3 = (f32[8,256,128]{2,1,0:T(8,128)S(1)}, f32[8,256,128]{2,1,0:T(8,128)S(1)}, u32[]{:S(2)}, u32[]{:S(2)}) collective-permute-start(f32[8,256,128]{2,1,0:T(8,128)S(1)} %fusion.5.refs_1_), channel_id=1, source_target_pairs={{0,4},{4,8},{8,12},{12,16},{16,20},{20,24},{24,28},{28,32},{32,36}... | collective-permute-start | bytes 3145736 | tf_op jit(solution)/shard_map/ppermute | solution.py:288
  43.2 16.1 %collective-permute-start.4 = (f32[8,256,128]{2,1,0:T(8,128)S(1)}, f32[8,256,128]{2,1,0:T(8,128)S(1)}, u32[]{:S(2)}, u32[]{:S(2)}) collective-permute-start(f32[8,256,128]{2,1,0:T(8,128)S(1)} %fusion.5.refs_1_), channel_id=1, source_target_pairs={{4,0},{8,4},{12,8},{16,12},{20,16},{24,20},{28,24},{32,28},{36,32}... | collective-permute-start | bytes 3145736 | tf_op jit(solution)/shard_map/ppermute | solution.py:288
